TPU v7x, 32 devices: a whole 2x2x4 slice. The times are simulated.
32 devices in a mesh: seq: 8 (over z, core), head: 4 (over y, x).
Axes of the slice: x: 2, y: 2, z: 4, core: 2. Of those that a mesh axis runs over, the one named last changes fastest.
Arguments:
- tokens: bfloat16 [2048, 4096], P('seq', 'head'), may hold values from -40 to 40
- norm_gain: float32 [4096], replicated, may hold values from 1.5 to 8
- w_qkv: bfloat16 [4096, 3, 512], P(None, None, 'head'), may hold values from -0.09375 to 0.09375
- w_out: bfloat16 [512, 4096], P('head'), may hold values from -0.75 to 0.75
- span_order: int32 [16], replicated, may hold values from 0 to 15, each once
- frame_id: int32 [2048], replicated, may hold values from 0 to 15, never falling along the last dimension, each value on 1 to 256 neighbouring positions
- camera_id: int32 [2048], replicated, may hold values from 0 to 5
Outputs:
- mixed: bfloat16 [2048, 4096], P('seq', 'head')
Inputs may be any that keep to these rules, and one draw needn't show every extreme that they name: `span_order`: each of the 16 spans appears once. `frame_id`: never falls along the sequence; every frame has 1 to 256 positions and one has exactly 256.
All inputs are finite; a program needn't handle non-finite values.
Results may differ from a plain program's by a relative error of at most 0.015.
The roundings to bfloat16 on the way count: a program that leaves them out, or rounds other values in their place, can miss the bound.
Values may be sent and summed in bfloat16 or wider, within the bound.
A program may use at most 64 MiB of HBM per device.

v0:
```python
import jax
import jax.numpy as jnp
from jax import lax
from jax.sharding import PartitionSpec as P

D = 4096
HD = 128


epsilon = 1e-06
key_block = 1024


def stored_order(id_table, span_order):
    span_count = span_order.shape[0]
    return id_table.reshape(span_count, -1)[span_order].reshape(-1)


def visible_pairs(query_frames, query_cameras, key_frames, key_cameras):
    earlier = key_frames[None, :] < query_frames[:, None]
    same_view = (key_frames[None, :] == query_frames[:, None]) & (
        key_cameras[None, :] == query_cameras[:, None]
    )
    return earlier | same_view


def on_device(tokens, norm_gain, w_qkv, w_out, span_order, frame_id, camera_id):
    gathered = lax.all_gather(tokens, "head", axis=1, tiled=True)
    widened = gathered.astype(jnp.float32)
    inverse = lax.rsqrt(jnp.mean(widened * widened, axis=1, keepdims=True) + epsilon)
    normed = (widened * inverse * norm_gain).astype(jnp.bfloat16)
    row_count = tokens.shape[0]
    local_heads = w_out.shape[0] // HD
    projected = jnp.dot(
        normed, w_qkv.reshape(D, 3 * local_heads * HD), preferred_element_type=jnp.float32
    )
    projected = projected.astype(jnp.bfloat16).reshape(row_count, 3, local_heads, HD)
    queries = projected[:, 0]
    key_rows = projected[:, 1].reshape(row_count, local_heads * HD)
    value_rows = projected[:, 2].reshape(row_count, local_heads * HD)
    frames = stored_order(frame_id, span_order)
    cameras = stored_order(camera_id, span_order)
    first_row = lax.axis_index("seq") * row_count
    query_frames = lax.dynamic_slice_in_dim(frames, first_row, row_count, 0)
    query_cameras = lax.dynamic_slice_in_dim(cameras, first_row, row_count, 0)
    score_scale = HD ** (-0.5)

    def absorb(running, block_keys, block_values, key_start, frame_table, camera_table):
        key_count = block_keys.shape[0]
        key_frames = lax.dynamic_slice_in_dim(frame_table, key_start, key_count, 0)
        key_cameras = lax.dynamic_slice_in_dim(camera_table, key_start, key_count, 0)
        old_best, running_total, weighted = running
        scores = (
            jnp.einsum(
                "qhd,khd->hqk",
                queries,
                block_keys.reshape(key_count, local_heads, HD),
                preferred_element_type=jnp.float32,
            )
            * score_scale
        )
        allowed = visible_pairs(query_frames, query_cameras, key_frames, key_cameras)[None]
        block_best = jnp.max(jnp.where(allowed, scores, -jnp.inf), axis=2)
        new_best = jnp.maximum(old_best, block_best)
        weights = jnp.exp(jnp.where(allowed, scores - new_best[:, :, None], -jnp.inf))
        factor = jnp.exp(old_best - new_best)
        running_total = running_total * factor + jnp.sum(weights, axis=2)
        added = jnp.einsum(
            "hqk,khd->hqd",
            weights.astype(jnp.bfloat16),
            block_values.reshape(key_count, local_heads, HD),
            preferred_element_type=jnp.float32,
        )
        weighted = weighted * factor[:, :, None] + added
        return (new_best, running_total, weighted)

    initial = (
        jnp.full((local_heads, row_count), -1e30, jnp.float32),
        jnp.zeros((local_heads, row_count), jnp.float32),
        jnp.zeros((local_heads, row_count, HD), jnp.float32),
    )
    all_keys, all_values = (
        lax.all_gather(key_rows, "seq", axis=0, tiled=True),
        lax.all_gather(value_rows, "seq", axis=0, tiled=True),
    )
    running = initial
    length = all_keys.shape[0]
    block_rows = min(key_block, length)
    full_blocks = length // block_rows

    def advance(block_index, current):
        offset = block_index * block_rows
        block_keys = lax.dynamic_slice_in_dim(all_keys, offset, block_rows, 0)
        block_values = lax.dynamic_slice_in_dim(all_values, offset, block_rows, 0)
        return absorb(current, block_keys, block_values, 0 + offset, frames, cameras)

    running = lax.fori_loop(0, full_blocks, advance, running)
    attended = (running[2] / running[1][:, :, None]).astype(jnp.bfloat16)
    partial_value = jnp.einsum(
        "hqd,hde->qe",
        attended,
        w_out.reshape(local_heads, HD, D),
        preferred_element_type=jnp.float32,
    )
    mixed_rows = lax.psum_scatter(
        partial_value.astype(jnp.bfloat16), "head", scatter_dimension=1, tiled=True
    )
    return mixed_rows


def solution(mesh):
    placed = (P("seq", "head"), P(), P(None, None, "head"), P("head", None), P(), P(), P())
    return jax.shard_map(
        on_device, mesh=mesh, in_specs=placed, out_specs=P("seq", "head"), check_vma=False
    )
```

profile of v0, /device:TPU:0, one launch (start us, length us, event | category | flops | bytes accessed | tf_op | source)
XLA Modules:
  0.0 131.8 jit_solution(4078720946869404674)
XLA Ops:
  6.5 0.0 copy-start
  6.5 0.0 all-gather.4.cloned.1.call-start
  6.5 0.7 all-gather.4.cloned.1.call-update
  7.3 0.0 reduce-scatter.2.cloned.1.call-start
  7.3 0.7 compare_select_fusion
  8.0 1.3 gather_fusion
  9.3 1.3 gather_fusion.1
  10.5 0.1 dynamic_slice.34
  10.6 0.1 dynamic_slice.35
  10.7 0.0 copy-start.1
  10.7 4.7 %copy.11 = bf16[4096,3,128]{0,2,1:T(8,128)(2,1)} copy(bf16[4096,3,128]{2,0,1:T(8,128)(2,1)} %param.11) | data formatting | bytes 6291456 | tf_op args[2]
  15.4 31.8 %all-gather.4.cloned.1.call-done = bf16[256,4096]{1,0:T(8,128)(2,1)} async-done(((bf16[256,1024]{1,0:T(8,128)(2,1)}), bf16[256,4096]{1,0:T(8,128)(2,1)}) %all-gather.4.cloned.1.call-update) | async-done | bytes 2097168 | tf_op jit(solution)/shard_map/all_gather | solution.py:28
  47.3 2.1 %fusion.16 = f32[256]{0:T(256)S(1)} fusion(bf16[256,4096]{1,0:T(8,128)(2,1)} %all-gather.4.cloned.1.call-done), kind=kLoop, calls=%fused_computation.29 | loop fusion | flops 3145472 | bytes 2098176 | tf_op jit(solution)/shard_map/reduce_sum | solution.py:30
  49.3 0.0 copy-done.1
  49.4 3.8 %fusion.23 = bf16[256,384]{1,0:T(8,128)(2,1)S(1)} fusion(bf16[4096,384]{0,1:T(8,128)(2,1)} %bitcast.42, bf16[256,4096]{1,0:T(8,128)(2,1)} %all-gather.4.cloned.1.call-done, f32[4096]{0:T(1024)S(1)} %copy-done.1, f32[256]{0:T(256)S(1)} %add_rsqrt_fusion), kind=kOutput, calls=%fused_computation.35 | convolution fusion | flops 809598976 | bytes 5456896 | tf_op jit(solution)/shard_map/dot_general | solution.py:34
  53.2 0.1 copy.12
  53.4 14.8 %all-gather = bf16[2048,1,1,128]{0,3,1,2:T(8,128)(2,1)S(1)} all-gather(bf16[256,1,1,128]{0,3,1,2:T(8,128)(2,1)S(1)} %get-tuple-element.267), channel_id=2, replica_groups=mesh['seq'=8,'head'=4] {'seq'}, dimensions={0}, use_global_device_ids=true | all-gather | bytes 589824 | tf_op jit(solution)/shard_map/all_gather | solution.py:83
  68.1 14.8 %all-gather.1 = bf16[2048,1,1,128]{0,3,1,2:T(8,128)(2,1)S(1)} all-gather(bf16[256,1,1,128]{0,3,1,2:T(8,128)(2,1)S(1)} %get-tuple-element.265), channel_id=3, replica_groups=mesh['seq'=8,'head'=4] {'seq'}, dimensions={0}, use_global_device_ids=true | all-gather | bytes 589824 | tf_op jit(solution)/shard_map/all_gather | solution.py:84
  82.9 0.1 copy.13
  83.0 4.0 %while.18 = (s32[]{:T(128)}, f32[1,256]{1,0:T(1,128)S(1)}, f32[1,256]{1,0:T(1,128)S(1)}, f32[1,256,128]{2,1,0:T(8,128)S(1)}, s32[2048]{0:T(1024)S(1)}, /*index=5...) while((s32[]{:T(128)}, f32[1,256]{1,0:T(1,128)S(1)}, ...), condition=%wide.region_4.5_spmd.clone, body=%wide.region_1.4_spmd.clone.sunk | while | flops 140608768 | bytes 4061399 | solution.py:97
  83.1 0.5 select_reduce_fusion.2
  83.6 0.7 fusion.39
  84.3 0.7 fusion.41
  85.0 0.5 select_reduce_fusion.2
  85.6 0.7 fusion.39
  86.3 0.7 fusion.41
  87.0 0.0 copy-done
  87.0 2.1 %convolution_convert_fusion = bf16[256,4096]{1,0:T(8,128)(2,1)} fusion(bf16[128,4096]{1,0:T(8,128)(2,1)S(1)} %copy-done, f32[1,256,128]{2,1,0:T(8,128)S(1)} %get-tuple-element.190, f32[256]{0:T(256)S(1)} %bitcast.56), kind=kOutput, calls=%fused_computation.28 | convolution fusion | flops 269549568 | bytes 3277824 | tf_op jit(solution)/shard_map/hqd,hde->qe/dot_general | solution.py:99
  89.1 0.0 reduce-scatter.2.cloned.1.call-update
  89.1 35.9 %reduce-scatter.2.cloned.1.call-done = bf16[256,1024]{1,0:T(8,128)(2,1)} async-done(((bf16[256,4096]{1,0:T(8,128)(2,1)}), bf16[256,1024]{1,0:T(8,128)(2,1)}) %reduce-scatter.2.cloned.1.call-update) | async-done | bytes 524304 | tf_op jit(solution)/shard_map/reduce_scatter | solution.py:105
  (16 shorter events, 0.1 us)
Async XLA Ops:
  6.5 80.4 %copy-start = (bf16[128,4096]{1,0:T(8,128)(2,1)S(1)}, bf16[128,4096]{1,0:T(8,128)(2,1)}, u32[]{:S(2)}) copy-start(bf16[128,4096]{1,0:T(8,128)(2,1)} %param.12) | copy-start | bytes 3145732
  6.5 40.7 %all-gather.4.cloned.1.call-start = ((), (), s32[]{:S(2)}) async-start(), calls=%async_computation.1 | async-start | bytes 2621440 | tf_op jit(solution)/shard_map/all_gather | solution.py:28
  7.3 117.7 %reduce-scatter.2.cloned.1.call-start = ((), (), s32[]{:S(2)}) async-start(), calls=%async_computation.2 | async-start | bytes 2621440 | tf_op jit(solution)/shard_map/reduce_scatter | solution.py:105
  10.7 38.7 %copy-start.1 = (f32[4096]{0:T(1024)S(1)}, f32[4096]{0:T(1024)}, u32[]{:S(2)}) copy-start(f32[4096]{0:T(1024)} %param.10) | copy-start | bytes 49156
Sparse Core Ops, SparseCore 0:
  9.2 38.0 all-gather.3
  89.2 35.6 reduce-scatter.1
where the time goes:
time: 132 us
  waiting for transfers between devices  68.4 us (52%)
  blocking collectives  29.5 us (22%)
  between operations  13.5 us (10%)
  matrix products  8.31 us (6%)
  local copies, waits for them, and re-layouts  7.71 us (6%)
  other arithmetic  4.17 us (3%)
    reduce_scatter x1, waiting for transfers between devices, on_device(): lax.psum_scatter(partial_value.astype(jnp.bfloat16), 'head', scatter_dime...  35.9 us
    all_gather x1, waiting for transfers between devices, on_device(): gathered = lax.all_gather(tokens, 'head', axis=1, tiled=True)  31.8 us
    all_gather x1, blocking collectives, on_device(): lax.all_gather(value_rows, 'seq', axis=0, tiled=True)  14.8 us
    all_gather x1, blocking collectives, on_device(): lax.all_gather(key_rows, 'seq', axis=0, tiled=True)  14.8 us
    unnamed x5, local copies, waits for them, and re-layouts  4.73 us
    dot_general x1, matrix products, on_device(): jnp.dot(normed, w_qkv.reshape(D, 3 * local_heads * HD), preferred_element...  3.82 us
  transfers between devices with their start and end apart: 2, of which 2 were waited for; matrix products, arithmetic and copies ran while one was open for 6% of the time, Pallas kernels for 0%

commit v1 on v0

v1 whole, which is shorter than its diff:
```python
import functools
import math

import jax
import jax.numpy as jnp
from jax import lax
from jax.experimental import pallas as pl
from jax.experimental.pallas import tpu as pltpu
from jax.sharding import PartitionSpec as P

HD = 128
EPSILON = 1e-06
CHUNKS = 4
CODE = 1024
MESH = pl.DeviceIdType.MESH


def kernel(
    n_seq, n_head, tokens, gain, w_qkv, w_out, spans, frames, cameras, out,
    gathered, w_vmem, codes, queries, kv, w_all, att, acc, run_m, run_l, run_o,
    local_sem, t_send, t_recv, f_send, k_send, k_recv, r_send, w_send, w_recv, v_send, a_send, a_recv,
):
    seq, head = lax.axis_index("seq"), lax.axis_index("head")
    rows, width = tokens.shape
    half = width // 2
    part = rows // CHUNKS
    minor_n = n_head // max(k for k in range(1, math.isqrt(n_head) + 1) if n_head % k == 0)
    major_n = n_head // minor_n
    major, minor = head // minor_n, lax.rem(head, minor_n)
    core, layer = lax.rem(seq, 2), seq // 2
    layers = n_seq // 2
    sibling = layer * 2 + 1 - core
    minor_peers = [major * minor_n + lax.rem(minor + k, minor_n) for k in range(1, minor_n)]
    major_peers = [lax.rem(major + k, major_n) * minor_n + minor for k in range(1, major_n)]
    far_peers = [
        lax.rem(major + i, major_n) * minor_n + lax.rem(minor + k, minor_n)
        for i in range(1, major_n) for k in range(1, minor_n)
    ]
    head_peers = minor_peers + major_peers + far_peers
    layer_peers = [lax.rem(layer + k, layers) * 2 + core for k in range(1, layers)]
    sent = []

    def send(src, dst, send_sem, recv_sem, device):
        copy = pltpu.make_async_remote_copy(
            src_ref=src, dst_ref=dst, send_sem=send_sem, recv_sem=recv_sem,
            device_id=device, device_id_type=MESH,
        )
        copy.start()
        sent.append(copy)

    def arrived(dst, recv_sem):
        pltpu.make_async_remote_copy(
            src_ref=dst, dst_ref=dst, send_sem=recv_sem, recv_sem=recv_sem,
            device_id={"seq": sibling}, device_id_type=MESH,
        ).wait_recv()

    def token_slot(c, j, origin):
        column = pl.multiple_of(origin * width + j * half, 128)
        return gathered.at[pl.ds(c * part, part), pl.ds(column, half)]

    def kv_slot(c, origin):
        return kv.at[c, pl.ds(pl.multiple_of(origin * part, part), part), :]

    def w_slot(origin, j):
        first = pl.multiple_of(origin * HD + j * (HD // 2), HD // 2)
        return w_all.at[pl.ds(first, HD // 2), :]

    def own_tokens(c):
        for j in range(2):
            src = tokens.at[pl.ds(c * part, part), pl.ds(j * half, half)]
            near = minor_peers + major_peers if j == 0 else major_peers + minor_peers
            for i, peer in enumerate(near):
                send(src, token_slot(c, j, head), t_send.at[c, j, i], t_recv.at[c, j, head], {"head": peer})

    def forward_tokens(c):
        for j, (sources, targets) in enumerate(((minor_peers, major_peers), (major_peers, minor_peers))):
            for i, origin in enumerate(sources):
                slot = token_slot(c, j, origin)
                arrived(slot, t_recv.at[c, j, origin])
                for k, peer in enumerate(targets):
                    send(slot, slot, f_send.at[c, j, i * len(targets) + k], t_recv.at[c, j, origin], {"head": peer})

    def project(c):
        for j, late in enumerate((major_peers + far_peers, minor_peers + far_peers)):
            for origin in late:
                arrived(token_slot(c, j, origin), t_recv.at[c, j, origin])
        here = pl.ds(c * part, part)
        wide = gathered[here, :].astype(jnp.float32)
        inverse = lax.rsqrt(jnp.mean(wide * wide, axis=1, keepdims=True) + EPSILON)
        normed = (wide * inverse * gain[...]).astype(jnp.bfloat16)
        projected = jnp.dot(normed, w_vmem[...], preferred_element_type=jnp.float32).astype(jnp.bfloat16)
        queries[here, :] = projected[:, :HD]
        slot = kv_slot(c, seq)
        slot[...] = projected[:, HD:]
        for i, peer in enumerate(layer_peers):
            send(slot, slot, k_send.at[c, i], k_recv.at[c, seq], {"seq": peer})
        send(slot, slot, k_send.at[c, layers - 1], k_recv.at[c, seq], {"seq": sibling})

    def relay(c):
        for i, origin in enumerate(layer_peers):
            slot = kv_slot(c, origin)
            arrived(slot, k_recv.at[c, origin])
            send(slot, slot, r_send.at[c, i], k_recv.at[c, origin], {"seq": sibling})

    def others(c):
        for k in range(layers):
            origin = lax.rem(layer + k, layers) * 2 + 1 - core
            arrived(kv_slot(c, origin), k_recv.at[c, origin])

    barrier = pltpu.get_barrier_semaphore()
    for peer in head_peers:
        pl.semaphore_signal(barrier, inc=1, device_id={"head": peer}, device_id_type=MESH)
    for peer in layer_peers + [sibling]:
        pl.semaphore_signal(barrier, inc=1, device_id={"seq": peer}, device_id_type=MESH)
    pl.semaphore_wait(barrier, len(head_peers) + len(layer_peers) + 1)

    own_tokens(0)
    own_tokens(1)
    local = [
        pltpu.make_async_copy(w_qkv.at[j], w_vmem.at[:, pl.ds(j * HD, HD)], local_sem.at[j]) for j in range(3)
    ]
    local.append(pltpu.make_async_copy(
        tokens, gathered.at[:, pl.ds(pl.multiple_of(head * width, 128), width)], local_sem.at[3]))
    local.append(pltpu.make_async_copy(
        w_out.at[:, pl.ds(pl.multiple_of(head * width, 128), width)],
        w_all.at[pl.ds(pl.multiple_of(head * HD, HD), HD), :], local_sem.at[4]))
    for copy in local:
        copy.start()

    span_count, span = frames.shape
    for s in range(span_count):
        place = spans[s]
        codes[pl.ds(s, 1), :] = frames[pl.ds(place, 1), :] * CODE + cameras[pl.ds(place, 1), :]
    own_spans = rows // span
    query_codes = jnp.concatenate([
        jnp.broadcast_to(codes[pl.ds(seq * own_spans + i, 1), :], (HD, span)).T for i in range(own_spans)
    ], axis=0)[:, :1]
    query_bases = query_codes - jnp.bitwise_and(query_codes, CODE - 1)
    for copy in local:
        copy.wait()

    for c in range(CHUNKS):
        forward_tokens(c)
        if c + 2 < CHUNKS:
            own_tokens(c + 2)
        if c + 1 == CHUNKS:
            for i, peer in enumerate(head_peers):
                src = w_out.at[pl.ds(pl.multiple_of(core * (HD // 2), HD // 2), HD // 2),
                               pl.ds(pl.multiple_of(peer * width, 128), width)]
                send(src, w_slot(head, core), w_send.at[i], w_recv.at[head, core], {"head": peer})
        if c >= 1:
            project(c - 1)
        if c >= 2:
            relay(c - 2)
    project(CHUNKS - 1)
    relay(CHUNKS - 2)

    scale = HD ** -0.5
    run_m[...] = jnp.full(run_m.shape, -1e30, jnp.float32)
    run_l[...] = jnp.zeros(run_l.shape, jnp.float32)
    run_o[...] = jnp.zeros(run_o.shape, jnp.float32)

    def absorb(c):
        pieces = []
        for d in range(n_seq):
            first = d * rows + c * part
            lane = first % span
            pieces.append(codes[first // span:first // span + 1, lane:lane + part])
        key_codes = jnp.concatenate(pieces, axis=1)
        allowed = (key_codes == query_codes) | (key_codes < query_bases)
        scores = lax.dot_general(
            queries[...], kv[c, :, :HD], (((1,), (1,)), ((), ())), preferred_element_type=jnp.float32
        ) * scale
        scores = jnp.where(allowed, scores, -jnp.inf)
        old = run_m[...]
        best = jnp.maximum(old, jnp.max(scores, axis=1, keepdims=True))
        weights = jnp.exp(scores - best)
        factor = jnp.exp(old - best)
        run_m[...] = best
        run_l[...] = run_l[...] * factor + jnp.sum(weights, axis=1, keepdims=True)
        run_o[...] = run_o[...] * factor + jnp.dot(
            weights.astype(jnp.bfloat16), kv[c, :, HD:], preferred_element_type=jnp.float32)

    for c in range(CHUNKS - 1):
        others(c)
        absorb(c)
    relay(CHUNKS - 1)
    for i, origin in enumerate(head_peers):
        slot = w_slot(origin, core)
        arrived(slot, w_recv.at[origin, core])
        send(slot, slot, v_send.at[i], w_recv.at[origin, core], {"seq": sibling})
    others(CHUNKS - 1)
    absorb(CHUNKS - 1)
    att[head] = (run_o[...] / run_l[...]).astype(jnp.bfloat16)
    for i, peer in enumerate(head_peers):
        send(att.at[head], att.at[head], a_send.at[i], a_recv.at[head], {"head": peer})

    def head_out(origin):
        w_rows = w_all[pl.ds(pl.multiple_of(origin * HD, HD), HD), :]
        return jnp.dot(att[origin], w_rows, preferred_element_type=jnp.float32).astype(jnp.bfloat16).astype(jnp.float32)

    acc[...] = head_out(head)
    for i, origin in enumerate(head_peers):
        arrived(w_slot(origin, 1 - core), w_recv.at[origin, 1 - core])
        arrived(att.at[origin], a_recv.at[origin])
        if i + 1 < len(head_peers):
            acc[...] += head_out(origin)
        else:
            out[...] = (acc[...] + head_out(origin)).astype(jnp.bfloat16)
    for copy in sent:
        copy.wait_send()


def on_device(n_seq, n_head, tokens, norm_gain, w_qkv, w_out, span_order, frame_id, camera_id):
    rows, width = tokens.shape
    depth = norm_gain.shape[0]
    part = rows // CHUNKS
    spans = span_order.shape[0]
    vmem, smem, hbm = (pl.BlockSpec(memory_space=m) for m in (pltpu.VMEM, pltpu.SMEM, pl.ANY))
    dma = pltpu.SemaphoreType.DMA
    keys = n_seq * rows
    return pl.pallas_call(
        functools.partial(kernel, n_seq, n_head),
        out_shape=jax.ShapeDtypeStruct((rows, width), jnp.bfloat16),
        in_specs=[hbm, vmem, hbm, hbm, smem, vmem, vmem],
        out_specs=vmem,
        scratch_shapes=[
            pltpu.VMEM((rows, depth), jnp.bfloat16),
            pltpu.VMEM((depth, 3 * HD), jnp.bfloat16),
            pltpu.VMEM((spans, keys // spans), jnp.int32),
            pltpu.VMEM((rows, HD), jnp.bfloat16),
            pltpu.VMEM((CHUNKS, n_seq * part, 2 * HD), jnp.bfloat16),
            pltpu.VMEM((n_head * HD, width), jnp.bfloat16),
            pltpu.VMEM((n_head, rows, HD), jnp.bfloat16),
            pltpu.VMEM((rows, width), jnp.float32),
            pltpu.VMEM((rows, 1), jnp.float32),
            pltpu.VMEM((rows, 1), jnp.float32),
            pltpu.VMEM((rows, HD), jnp.float32),
            dma((5,)),
            dma((CHUNKS, 2, n_head)),
            dma((CHUNKS, 2, n_head)),
            dma((CHUNKS, 2, n_head)),
            dma((CHUNKS, n_seq // 2)),
            dma((CHUNKS, n_seq)),
            dma((CHUNKS, n_seq // 2)),
            dma((n_head,)),
            dma((n_head, 2)),
            dma((n_head,)),
            dma((n_head,)),
            dma((n_head,)),
        ],
        compiler_params=pltpu.CompilerParams(
            collective_id=0, has_side_effects=True, vmem_limit_bytes=48 * 1024 * 1024
        ),
    )(
        tokens, norm_gain.reshape(1, depth), w_qkv.transpose(1, 0, 2), w_out, span_order,
        frame_id.reshape(spans, -1), camera_id.reshape(spans, -1),
    )


def solution(mesh):
    placed = (P("seq", "head"), P(), P(None, None, "head"), P("head", None), P(), P(), P())
    body = functools.partial(on_device, mesh.shape["seq"], mesh.shape["head"])
    return jax.shard_map(body, mesh=mesh, in_specs=placed, out_specs=P("seq", "head"), check_vma=False)
```

time: 132 us -> 47.7 us (0.36)
  waiting for transfers between devices: 68.4 us -> 0 us
  Pallas kernels: 0 us -> 39.6 us
  blocking collectives: 29.5 us -> 0 us
  between operations: 13.5 us -> 0.02 us
  matrix products: 8.31 us -> 0 us
  other arithmetic: 4.17 us -> 0 us
    pallas_call x0 -> x1, Pallas kernels: none -> 39.6 us  [on_device(): pl.pallas_call(functools.partial(kernel, n_seq, n_head), out_shape=jax.Sh...]
    reduce_scatter x1 -> x0, waiting for transfers between devices: 35.9 us -> none  [on_device(): lax.psum_scatter(partial_value.astype(jnp.bfloat16), 'head', scatter_dime...]
    all_gather x1 -> x0, waiting for transfers between devices: 31.8 us -> none  [on_device(): gathered = lax.all_gather(tokens, 'head', axis=1, tiled=True)]
    all_gather x2 -> x0, blocking collectives: 29.5 us -> none  [the longest x1 14.8 us: on_device(): lax.all_gather(value_rows, 'seq', axis=0, tiled=True)]
    dot_general x6 -> x0, matrix products: 8.31 us -> none  [the longest x1 3.82 us: on_device(): jnp.dot(normed, w_qkv.reshape(D, 3 * local_heads * HD), preferred_element...]
    reduce_sum x3 -> x0, other arithmetic: 3.44 us -> none  [the longest x1 2.08 us: on_device(): jnp.mean(widened * widened, axis=1, keepdims=True) + epsilon]
    unnamed x5 -> x15, local copies, waits for them, and re-layouts: 4.73 us -> 7.71 us
    gather x2 -> x0, local copies, waits for them, and re-layouts: 2.52 us -> none  [stored_order(): return id_table.reshape(span_count, -1)[span_order].reshape(-1)]
  transfers between devices with their start and end apart: 2 -> 0, of which waited for: 2 -> 0; matrix products, arithmetic and copies ran while one was open for 6% -> 0% of each run, Pallas kernels for 0% -> 0%
where the time goes in v1:
time: 47.7 us; the launch traced here: 47.3 us
  Pallas kernels  39.6 us (83%)
  local copies, waits for them, and re-layouts  7.71 us (16%)
    pallas_call x1, Pallas kernels, on_device(): pl.pallas_call(functools.partial(kernel, n_seq, n_head), out_shape=jax.Sh...  39.6 us
    unnamed x15, local copies, waits for them, and re-layouts  7.71 us

profile of v1, /device:TPU:0, one launch (start us, length us, event | category | flops | bytes accessed | tf_op | source)
XLA Modules:
  0.0 47.3 jit_solution(7837323430406529253)
XLA Ops:
  0.0 0.0 copy-start
  0.0 1.9 %copy-done = bf16[4096,3,128]{2,0,1:T(8,128)(2,1)S(1)} copy-done((bf16[4096,3,128]{2,0,1:T(8,128)(2,1)S(1)}, bf16[4096,3,128]{2,0,1:T(8,128)(2,1)}, u32[]{:S(2)}) %copy-start) | copy-done | bytes 3145752
  1.9 0.0 copy-start.1
  1.9 1.2 %copy-done.1 = bf16[128,4096]{1,0:T(8,128)(2,1)S(1)} copy-done((bf16[128,4096]{1,0:T(8,128)(2,1)S(1)}, bf16[128,4096]{1,0:T(8,128)(2,1)}, u32[]{:S(2)}) %copy-start.1) | copy-done | bytes 1048600
  3.1 0.0 copy-start.2
  3.1 1.0 %copy-done.2 = bf16[256,1024]{1,0:T(8,128)(2,1)S(1)} copy-done((bf16[256,1024]{1,0:T(8,128)(2,1)S(1)}, bf16[256,1024]{1,0:T(8,128)(2,1)}, u32[]{:S(2)}) %copy-start.2) | copy-done | bytes 524312
  4.2 0.0 copy-start.3
  4.2 0.7 %copy-done.3 = f32[4096]{0:T(1024)S(1)} copy-done((f32[4096]{0:T(1024)S(1)}, f32[4096]{0:T(1024)}, u32[]{:S(2)}) %copy-start.3) | copy-done | bytes 16408
  4.9 0.0 copy-start.4
  4.9 0.7 %copy-done.4 = s32[2048]{0:T(1024)S(1)} copy-done((s32[2048]{0:T(1024)S(1)}, s32[2048]{0:T(1024)}, u32[]{:S(2)}) %copy-start.4) | copy-done | bytes 8216
  5.6 0.0 copy-start.5
  5.6 0.7 %copy-done.5 = s32[2048]{0:T(1024)S(1)} copy-done((s32[2048]{0:T(1024)S(1)}, s32[2048]{0:T(1024)}, u32[]{:S(2)}) %copy-start.5) | copy-done | bytes 8216
  6.3 0.0 copy-start.6
  6.3 0.7 %copy-done.6 = s32[16]{0:T(128)S(1)} copy-done((s32[16]{0:T(128)S(1)}, s32[16]{0:T(128)}, u32[]{:S(2)}) %copy-start.6) | copy-done | bytes 88
  6.9 39.6 %shard_map.73 = bf16[256,1024]{1,0:T(8,128)(2,1)S(1)} custom-call(bf16[256,1024]{1,0:T(8,128)(2,1)S(1)} %copy-done.2, f32[1,4096]{1,0:T(1,128)S(1)} %bitcast.5, bf16[3,4096,128]{2,1,0:T(8,128)(2,1)S(1)} %bitcast.4, bf16[128,4096]{1,0:T(8,128)(2,1)S(1)} %copy-done.1, s32[16]{0:T(128)S(1)} %copy-done.6, s32[16,128]{1,0:T(8,128)S(1)} %bitcast.6, ...), custom_call_target="tpu_custom_call" | custom-call | tf_op jit(solution)/shard_map/pallas_call | solution.py:222
  46.5 0.8 %copy.9 = bf16[256,1024]{1,0:T(8,128)(2,1)} copy(bf16[256,1024]{1,0:T(8,128)(2,1)S(1)} %shard_map.73) | data formatting | bytes 1048576
Async XLA Ops:
  0.0 1.9 %copy-start = (bf16[4096,3,128]{2,0,1:T(8,128)(2,1)S(1)}, bf16[4096,3,128]{2,0,1:T(8,128)(2,1)}, u32[]{:S(2)}) copy-start(bf16[4096,3,128]{2,0,1:T(8,128)(2,1)} %param.9) | copy-start | bytes 9437188
  1.9 1.2 %copy-start.1 = (bf16[128,4096]{1,0:T(8,128)(2,1)S(1)}, bf16[128,4096]{1,0:T(8,128)(2,1)}, u32[]{:S(2)}) copy-start(bf16[128,4096]{1,0:T(8,128)(2,1)} %w_out.1) | copy-start | bytes 3145732
  3.1 1.0 %copy-start.2 = (bf16[256,1024]{1,0:T(8,128)(2,1)S(1)}, bf16[256,1024]{1,0:T(8,128)(2,1)}, u32[]{:S(2)}) copy-start(bf16[256,1024]{1,0:T(8,128)(2,1)} %tokens.1) | copy-start | bytes 1572868
  4.2 0.7 %copy-start.3 = (f32[4096]{0:T(1024)S(1)}, f32[4096]{0:T(1024)}, u32[]{:S(2)}) copy-start(f32[4096]{0:T(1024)} %param.8) | copy-start | bytes 49156
  4.9 0.7 %copy-start.4 = (s32[2048]{0:T(1024)S(1)}, s32[2048]{0:T(1024)}, u32[]{:S(2)}) copy-start(s32[2048]{0:T(1024)} %param.12) | copy-start | bytes 24580
  5.6 0.7 %copy-start.5 = (s32[2048]{0:T(1024)S(1)}, s32[2048]{0:T(1024)}, u32[]{:S(2)}) copy-start(s32[2048]{0:T(1024)} %param.13) | copy-start | bytes 24580
  6.3 0.7 %copy-start.6 = (s32[16]{0:T(128)S(1)}, s32[16]{0:T(128)}, u32[]{:S(2)}) copy-start(s32[16]{0:T(128)} %spans.1) | copy-start | bytes 196

commit v2 on v1

--- a/solution.py
+++ b/solution.py
@@ -10,20 +10,22 @@
 
 HD = 128
 EPSILON = 1e-06
-CHUNKS = 4
+SHARES = (1, 1, 1, 1)
+CHUNKS = len(SHARES)
 CODE = 1024
 MESH = pl.DeviceIdType.MESH
 
 
 def kernel(
-    n_seq, n_head, tokens, gain, w_qkv, w_out, spans, frames, cameras, out,
-    gathered, w_vmem, codes, queries, kv, w_all, att, acc, run_m, run_l, run_o,
+    n_seq, n_head, tokens, gain_in, w_qkv, w_out, spans_in, frames_in, cameras_in, out,
+    gain, spans, frames, cameras, gathered, w_vmem, codes, queries, kv, w_all, att, acc, run_m, run_l, run_o,
     local_sem, t_send, t_recv, f_send, k_send, k_recv, r_send, w_send, w_recv, v_send, a_send, a_recv,
 ):
     seq, head = lax.axis_index("seq"), lax.axis_index("head")
     rows, width = tokens.shape
     half = width // 2
-    part = rows // CHUNKS
+    sizes = [rows * share // sum(SHARES) for share in SHARES]
+    starts = [sum(sizes[:c]) for c in range(CHUNKS)]
     minor_n = n_head // max(k for k in range(1, math.isqrt(n_head) + 1) if n_head % k == 0)
     major_n = n_head // minor_n
     major, minor = head // minor_n, lax.rem(head, minor_n)
@@ -56,10 +58,11 @@
 
     def token_slot(c, j, origin):
         column = pl.multiple_of(origin * width + j * half, 128)
-        return gathered.at[pl.ds(c * part, part), pl.ds(column, half)]
+        return gathered.at[pl.ds(starts[c], sizes[c]), pl.ds(column, half)]
 
     def kv_slot(c, origin):
-        return kv.at[c, pl.ds(pl.multiple_of(origin * part, part), part), :]
+        first = pl.multiple_of(n_seq * starts[c] + origin * sizes[c], 16)
+        return kv.at[pl.ds(first, sizes[c]), :]
 
     def w_slot(origin, j):
         first = pl.multiple_of(origin * HD + j * (HD // 2), HD // 2)
@@ -67,7 +70,7 @@
 
     def own_tokens(c):
         for j in range(2):
-            src = tokens.at[pl.ds(c * part, part), pl.ds(j * half, half)]
+            src = tokens.at[pl.ds(starts[c], sizes[c]), pl.ds(j * half, half)]
             near = minor_peers + major_peers if j == 0 else major_peers + minor_peers
             for i, peer in enumerate(near):
                 send(src, token_slot(c, j, head), t_send.at[c, j, i], t_recv.at[c, j, head], {"head": peer})
@@ -84,7 +87,7 @@
         for j, late in enumerate((major_peers + far_peers, minor_peers + far_peers)):
             for origin in late:
                 arrived(token_slot(c, j, origin), t_recv.at[c, j, origin])
-        here = pl.ds(c * part, part)
+        here = pl.ds(starts[c], sizes[c])
         wide = gathered[here, :].astype(jnp.float32)
         inverse = lax.rsqrt(jnp.mean(wide * wide, axis=1, keepdims=True) + EPSILON)
         normed = (wide * inverse * gain[...]).astype(jnp.bfloat16)
@@ -112,10 +115,6 @@
         pl.semaphore_signal(barrier, inc=1, device_id={"head": peer}, device_id_type=MESH)
     for peer in layer_peers + [sibling]:
         pl.semaphore_signal(barrier, inc=1, device_id={"seq": peer}, device_id_type=MESH)
-    pl.semaphore_wait(barrier, len(head_peers) + len(layer_peers) + 1)
-
-    own_tokens(0)
-    own_tokens(1)
     local = [
         pltpu.make_async_copy(w_qkv.at[j], w_vmem.at[:, pl.ds(j * HD, HD)], local_sem.at[j]) for j in range(3)
     ]
@@ -124,8 +123,18 @@
     local.append(pltpu.make_async_copy(
         w_out.at[:, pl.ds(pl.multiple_of(head * width, 128), width)],
         w_all.at[pl.ds(pl.multiple_of(head * HD, HD), HD), :], local_sem.at[4]))
-    for copy in local:
+    small = [
+        pltpu.make_async_copy(src, dst, local_sem.at[5 + i])
+        for i, (src, dst) in enumerate(((spans_in, spans), (frames_in, frames), (cameras_in, cameras), (gain_in, gain)))
+    ]
+    for copy in small + local:
         copy.start()
+    pl.semaphore_wait(barrier, len(head_peers) + len(layer_peers) + 1)
+
+    own_tokens(0)
+    own_tokens(1)
+    for copy in small:
+        copy.wait()
 
     span_count, span = frames.shape
     for s in range(span_count):
@@ -136,9 +145,6 @@
         jnp.broadcast_to(codes[pl.ds(seq * own_spans + i, 1), :], (HD, span)).T for i in range(own_spans)
     ], axis=0)[:, :1]
     query_bases = query_codes - jnp.bitwise_and(query_codes, CODE - 1)
-    for copy in local:
-        copy.wait()
-
     for c in range(CHUNKS):
         forward_tokens(c)
         if c + 2 < CHUNKS:
@@ -148,6 +154,9 @@
                 src = w_out.at[pl.ds(pl.multiple_of(core * (HD // 2), HD // 2), HD // 2),
                                pl.ds(pl.multiple_of(peer * width, 128), width)]
                 send(src, w_slot(head, core), w_send.at[i], w_recv.at[head, core], {"head": peer})
+        if c == 1:
+            for copy in local:
+                copy.wait()
         if c >= 1:
             project(c - 1)
         if c >= 2:
@@ -163,13 +172,17 @@
     def absorb(c):
         pieces = []
         for d in range(n_seq):
-            first = d * rows + c * part
-            lane = first % span
-            pieces.append(codes[first // span:first // span + 1, lane:lane + part])
+            first, end = d * rows + starts[c], d * rows + starts[c] + sizes[c]
+            while first < end:
+                lane = first % span
+                count = min(end - first, span - lane)
+                pieces.append(codes[first // span:first // span + 1, lane:lane + count])
+                first += count
+        here = pl.ds(n_seq * starts[c], n_seq * sizes[c])
         key_codes = jnp.concatenate(pieces, axis=1)
         allowed = (key_codes == query_codes) | (key_codes < query_bases)
         scores = lax.dot_general(
-            queries[...], kv[c, :, :HD], (((1,), (1,)), ((), ())), preferred_element_type=jnp.float32
+            queries[...], kv[here, :HD], (((1,), (1,)), ((), ())), preferred_element_type=jnp.float32
         ) * scale
         scores = jnp.where(allowed, scores, -jnp.inf)
         old = run_m[...]
@@ -179,21 +192,21 @@
         run_m[...] = best
         run_l[...] = run_l[...] * factor + jnp.sum(weights, axis=1, keepdims=True)
         run_o[...] = run_o[...] * factor + jnp.dot(
-            weights.astype(jnp.bfloat16), kv[c, :, HD:], preferred_element_type=jnp.float32)
+            weights.astype(jnp.bfloat16), kv[here, HD:], preferred_element_type=jnp.float32)
 
     for c in range(CHUNKS - 1):
         others(c)
         absorb(c)
     relay(CHUNKS - 1)
-    for i, origin in enumerate(head_peers):
-        slot = w_slot(origin, core)
-        arrived(slot, w_recv.at[origin, core])
-        send(slot, slot, v_send.at[i], w_recv.at[origin, core], {"seq": sibling})
     others(CHUNKS - 1)
     absorb(CHUNKS - 1)
     att[head] = (run_o[...] / run_l[...]).astype(jnp.bfloat16)
     for i, peer in enumerate(head_peers):
         send(att.at[head], att.at[head], a_send.at[i], a_recv.at[head], {"head": peer})
+    for i, origin in enumerate(head_peers):
+        slot = w_slot(origin, core)
+        arrived(slot, w_recv.at[origin, core])
+        send(slot, slot, v_send.at[i], w_recv.at[origin, core], {"seq": sibling})
 
     def head_out(origin):
         w_rows = w_all[pl.ds(pl.multiple_of(origin * HD, HD), HD), :]
@@ -214,29 +227,32 @@
 def on_device(n_seq, n_head, tokens, norm_gain, w_qkv, w_out, span_order, frame_id, camera_id):
     rows, width = tokens.shape
     depth = norm_gain.shape[0]
-    part = rows // CHUNKS
     spans = span_order.shape[0]
-    vmem, smem, hbm = (pl.BlockSpec(memory_space=m) for m in (pltpu.VMEM, pltpu.SMEM, pl.ANY))
+    hbm = pl.BlockSpec(memory_space=pltpu.HBM)
     dma = pltpu.SemaphoreType.DMA
     keys = n_seq * rows
     return pl.pallas_call(
         functools.partial(kernel, n_seq, n_head),
         out_shape=jax.ShapeDtypeStruct((rows, width), jnp.bfloat16),
-        in_specs=[hbm, vmem, hbm, hbm, smem, vmem, vmem],
-        out_specs=vmem,
+        in_specs=[hbm] * 7,
+        out_specs=pl.BlockSpec(memory_space=pltpu.VMEM),
         scratch_shapes=[
+            pltpu.VMEM((1, depth), jnp.float32),
+            pltpu.SMEM((spans,), jnp.int32),
+            pltpu.VMEM((spans, keys // spans), jnp.int32),
+            pltpu.VMEM((spans, keys // spans), jnp.int32),
             pltpu.VMEM((rows, depth), jnp.bfloat16),
             pltpu.VMEM((depth, 3 * HD), jnp.bfloat16),
             pltpu.VMEM((spans, keys // spans), jnp.int32),
             pltpu.VMEM((rows, HD), jnp.bfloat16),
-            pltpu.VMEM((CHUNKS, n_seq * part, 2 * HD), jnp.bfloat16),
+            pltpu.VMEM((keys, 2 * HD), jnp.bfloat16),
             pltpu.VMEM((n_head * HD, width), jnp.bfloat16),
             pltpu.VMEM((n_head, rows, HD), jnp.bfloat16),
             pltpu.VMEM((rows, width), jnp.float32),
             pltpu.VMEM((rows, 1), jnp.float32),
             pltpu.VMEM((rows, 1), jnp.float32),
             pltpu.VMEM((rows, HD), jnp.float32),
-            dma((5,)),
+            dma((9,)),
             dma((CHUNKS, 2, n_head)),
             dma((CHUNKS, 2, n_head)),
             dma((CHUNKS, 2, n_head)),
@@ -250,7 +266,7 @@
             dma((n_head,)),
         ],
         compiler_params=pltpu.CompilerParams(
-            collective_id=0, has_side_effects=True, vmem_limit_bytes=48 * 1024 * 1024
+            collective_id=0, has_side_effects=True, vmem_limit_bytes=60 * 1024 * 1024
         ),
     )(
         tokens, norm_gain.reshape(1, depth), w_qkv.transpose(1, 0, 2), w_out, span_order,

time: 47.7 us -> 42 us (0.88)
  local copies, waits for them, and re-layouts: 7.71 us -> 1.87 us
    unnamed x15 -> x1, local copies, waits for them, and re-layouts: 7.71 us -> 1.87 us
where the time goes in v2:
time: 42 us; the launch traced here: 41.9 us
  Pallas kernels  40 us (95%)
  local copies, waits for them, and re-layouts  1.87 us (4%)
    pallas_call x1, Pallas kernels, on_device(): pl.pallas_call(functools.partial(kernel, n_seq, n_head), out_shape=jax.Sh...  40 us
    unnamed x1, local copies, waits for them, and re-layouts  1.87 us

profile of v2, /device:TPU:0, one launch (start us, length us, event | category | flops | bytes accessed | tf_op | source)
XLA Modules:
  0.0 41.9 jit_solution(11017480198656441122)
XLA Ops:
  0.0 40.0 %shard_map.73 = bf16[256,1024]{1,0:T(8,128)(2,1)} custom-call(bf16[256,1024]{1,0:T(8,128)(2,1)} %tokens.1, f32[1,4096]{1,0:T(1,128)} %bitcast.5, bf16[3,4096,128]{2,1,0:T(8,128)(2,1)} %bitcast.4, bf16[128,4096]{1,0:T(8,128)(2,1)} %w_out.1, s32[16]{0:T(128)} %spans_in.1, s32[16,128]{1,0:T(8,128)} %bitcast.6, s32[16,128]{1,0:T(8,128)} %bitcast.7), custom_call_target="tpu_custom_call" | custom-call | tf_op jit(solution)/shard_map/pallas_call | solution.py:234
  40.0 1.9 %copy.9 = bf16[256,1024]{1,0:T(8,128)(2,1)} copy(bf16[256,1024]{1,0:T(8,128)(2,1)} %shard_map.73) | data formatting | bytes 1048576
